TPU v7x, 128 devices: a whole 4x4x4 slice. The times are simulated.
128 devices in a mesh: gx: 8 (over x, core), gy: 16 (over z, y).
Axes of the slice: x: 4, y: 4, z: 4, core: 2. Of those that a mesh axis runs over, the one named last changes fastest.
Arguments:
- multipliers: bfloat16 [8, 16, 256, 2, 640], P('gx', 'gy'), may hold values from -6 to 6
- partner: int32 [8, 16, 2, 640], P('gx', 'gy'), may hold values from 0 to 639, each once within a row
- interface_rows: int32 [8, 16, 2608], P('gx', 'gy'), may hold values from 0 to 3071, as said below
- block_mask: int32 [8, 16, 16, 16], P('gx', 'gy'), may hold values 0 or 1
- tiles: bfloat16 [8, 16, 3072, 3072], P('gx', 'gy')
- basis: bfloat16 [8, 16, 48, 3072], P('gx', 'gy'), may hold values from -1.1953125 to 1.1953125
- coarse_inverse: bfloat16 [1536, 1536], replicated, may hold values from -0.15625 to 0.15625
Outputs:
- jumps: bfloat16 [8, 16, 256, 2, 640], P('gx', 'gy')
- curvature: float32 [256], replicated
Inputs may be any that keep to these rules, and one draw needn't show every extreme that they name: `interface_rows`: each subdomain's rows are distinct.
All inputs are finite; a program needn't handle non-finite values. No bound on the sum of `block_mask` on one device may be relied on, other than what follows from the above.
Results may differ from a plain program's by a relative error of at most 0.006.
Values may be sent and summed in bfloat16 or wider, within the bound.
A program may use at most 192 MiB of HBM per device.

v0:
```python
import jax
import jax.numpy as jnp
from jax import lax
from jax.sharding import PartitionSpec as P


def passed_along(block, axis, distance):
    devices = range(lax.axis_size(axis))
    route = [((i - distance) % len(devices), i) for i in devices]
    return lax.ppermute(block, axis, route)


def place(values, perm):
    return jnp.zeros_like(values).at[:, perm].set(values)


def shards(multipliers, partner, interface_rows, block_mask, tiles, basis, coarse_inverse):
    lam = multipliers[0, 0]
    pairs = partner[0, 0]
    rows = interface_rows[0, 0]
    mask = block_mask[0, 0]
    tile = tiles[0, 0]
    phi = basis[0, 0]
    nrhs, faces = (lam.shape[0], lam.shape[2])
    width = tile.shape[0]
    nblock = mask.shape[0]
    bsize = width // nblock
    corner_dofs = phi.shape[0] // 4
    count_x = lax.axis_size("gx")
    count_y = lax.axis_size("gy")
    row_a = lax.axis_index("gx")
    col_b = lax.axis_index("gy")
    total_coarse = coarse_inverse.shape[0]
    placed_east = place(lam[:, 0], pairs[0])
    placed_south = place(lam[:, 1], pairs[1])
    from_west = passed_along(placed_east, "gy", 1)
    from_north = passed_along(placed_south, "gx", 1)
    spread = jnp.zeros((nrhs, width), jnp.bfloat16)
    spread = spread.at[:, rows[3 * faces : 4 * faces]].set(lam[:, 0])
    spread = spread.at[:, rows[faces : 2 * faces]].set(lam[:, 1])
    spread = spread.at[:, rows[2 * faces : 3 * faces]].set(-from_west)
    spread = spread.at[:, rows[0:faces]].set(-from_north)
    masked = (
        tile.reshape(nblock, bsize, nblock, bsize) * mask.astype(jnp.bfloat16)[:, None, :, None]
    ).reshape(width, width)
    local_image = jnp.dot(spread, masked, preferred_element_type=jnp.float32)
    nodes = jnp.stack(
        [
            row_a * count_y + col_b,
            row_a * count_y + (col_b + 1) % count_y,
            (row_a + 1) % count_x * count_y + col_b,
            (row_a + 1) % count_x * count_y + (col_b + 1) % count_y,
        ]
    )
    columns = (
        nodes[:, None] * corner_dofs + jnp.arange(corner_dofs, dtype=jnp.int32)[None, :]
    ).reshape(-1)
    corner_load = local_image[:, rows[4 * faces :]]
    load_part = jnp.zeros((nrhs, total_coarse), jnp.float32).at[:, columns].add(corner_load)
    coarse_load = lax.psum(load_part, ("gx", "gy"))
    coarse_solution = jnp.dot(
        coarse_load.astype(jnp.bfloat16), coarse_inverse, preferred_element_type=jnp.float32
    )
    corner_values = coarse_solution[:, columns].astype(jnp.bfloat16)
    image = local_image - jnp.dot(corner_values, phi, preferred_element_type=jnp.float32)
    product_sum = lax.psum(jnp.sum(spread.astype(jnp.float32) * image, axis=1), ("gx", "gy"))
    face_values = image[:, rows[: 4 * faces]].astype(jnp.bfloat16).reshape(nrhs, 4, faces)
    east_west = passed_along(face_values[:, 2], "gy", -1)
    south_north = passed_along(face_values[:, 0], "gx", -1)
    jump_east = face_values[:, 3].astype(jnp.float32) - jnp.take(
        east_west, pairs[0], axis=1
    ).astype(jnp.float32)
    jump_south = face_values[:, 1].astype(jnp.float32) - jnp.take(
        south_north, pairs[1], axis=1
    ).astype(jnp.float32)
    jumps = jnp.stack([jump_east, jump_south], axis=1).astype(jnp.bfloat16)[None, None]
    curvature = product_sum / (2.0 * faces * count_x * count_y)
    return (jumps, curvature)


def solution(mesh):
    in_specs = (
        P("gx", "gy", None, None, None),
        P("gx", "gy", None, None),
        P("gx", "gy", None),
        P("gx", "gy", None, None),
        P("gx", "gy", None, None),
        P("gx", "gy", None, None),
        P(),
    )
    out_specs = (P("gx", "gy", None, None, None), P())
    return jax.shard_map(shards, mesh=mesh, in_specs=in_specs, out_specs=out_specs, check_vma=False)
```

profile of v0, /device:TPU:1, one launch (start us, length us, event | category | flops | bytes accessed | tf_op | source)
XLA Modules:
  0.0 288.4 jit_solution(1413179492641249364)
XLA Ops:
  0.6 0.0 copy-start
  0.6 0.0 copy-start.5
  0.7 1.2 copy.27
  1.9 0.0 copy-start.4
  1.9 0.1 slice_bitcast_fusion.4
  1.9 0.2 copy.18
  2.1 0.0 copy-done.5
  2.1 0.0 copy-start.6
  2.2 5.4 %scatter_custom_fusion.2 = bf16[256,640]{0,1:T(8,128)(2,1)S(1)} fusion(s32[640]{0:T(1024)S(1)} %get-tuple-element.14, bf16[640,256]{1,0:T(8,128)(2,1)S(1)} %copy.18, bf16[]{:T(256)} %constant.28.clone.1), kind=kCustom, calls=%fused_computation.45 | custom fusion | bytes 327682 | tf_op jit(solution)/shard_map/scatter | solution.py:14
  7.6 2.2 collective-permute-start
  9.8 0.2 copy.19
  10.0 5.4 %scatter_custom_fusion.4 = bf16[256,640]{0,1:T(8,128)(2,1)S(1)} fusion(s32[640]{0:T(1024)S(1)} %get-tuple-element.13, bf16[640,256]{1,0:T(8,128)(2,1)S(1)} %copy.19, bf16[]{:T(256)} %constant.28.clone.1), kind=kCustom, calls=%fused_computation.43 | custom fusion | bytes 327682 | tf_op jit(solution)/shard_map/scatter | solution.py:14
  15.5 2.1 collective-permute-start.1
  17.5 0.0 copy-done.4
  17.5 0.6 fusion.29
  18.2 0.6 fusion.32
  18.8 6.2 %scatter_custom_fusion = bf16[256,3072]{0,1:T(8,128)(2,1)S(1)} fusion(s32[640]{0:T(1024)} %get-tuple-element.10, bf16[640,256]{1,0:T(8,128)(2,1)S(1)} %copy.18, bf16[]{:T(256)} %constant.28.clone.1), kind=kCustom, calls=%fused_computation.20 | custom fusion | bytes 1573376 | tf_op jit(solution)/shard_map/scatter | solution.py:39
  25.0 0.0 copy-done.6
  25.0 8.6 %mul.30 = bf16[16,192,16,192]{3,2,1,0:T(8,128)(2,1)} broadcast(bf16[16,16]{1,0:T(8,128)(2,1)S(1)} %convert_bitcast_fusion), dimensions={0,2} | broadcast | bytes 18874880 | tf_op jit(solution)/shard_map/mul | solution.py:44
  33.6 0.0 copy-start.7
  33.6 39.2 %mul.31 = bf16[3072,3072]{1,0:T(8,128)(2,1)} reshape(bf16[16,192,16,192]{3,2,1,0:T(8,128)(2,1)} %mul.30) | data formatting | bytes 37748736 | tf_op jit(solution)/shard_map/mul | solution.py:44
  72.8 0.1 add_multiply_fusion
  72.9 0.1 iota_add_fusion
  73.0 0.1 add.179
  73.1 0.0 copy-done.7
  73.1 6.4 %scatter_fusion = bf16[256,3072]{0,1:T(8,128)(2,1)S(1)} fusion(bf16[256,3072]{0,1:T(8,128)(2,1)S(1)} %scatter_custom_fusion, s32[640]{0:T(1024)S(1)} %get-tuple-element.9, bf16[640,256]{1,0:T(8,128)(2,1)S(1)} %copy.19), kind=kCustom, calls=%fused_computation.6 | custom fusion | bytes 985600 | tf_op jit(solution)/shard_map/scatter | solution.py:40
  79.6 0.0 collective-permute-done
  79.6 6.7 %scatter_custom_fusion.3 = bf16[256,3072]{0,1:T(8,128)(2,1)S(1)} fusion(bf16[256,3072]{0,1:T(8,128)(2,1)S(1)} %scatter_fusion, s32[640]{0:T(1024)} %get-tuple-element.8, bf16[256,640]{0,1:T(8,128)(2,1)S(1)} %collective-permute-done), kind=kCustom, calls=%fused_computation.38 | custom fusion | flops 163840 | bytes 1900544 | tf_op jit(solution)/shard_map/scatter | solution.py:41
  86.3 0.0 collective-permute-done.1
  86.3 6.9 %scatter_custom_fusion.5 = bf16[256,3072]{0,1:T(8,128)(2,1)S(1)} fusion(bf16[256,3072]{0,1:T(8,128)(2,1)S(1)} %scatter_custom_fusion.3, s32[640]{0:T(1024)S(1)} %get-tuple-element.7, bf16[256,640]{0,1:T(8,128)(2,1)} %collective-permute-done.1), kind=kCustom, calls=%fused_computation.36 | custom fusion | flops 163840 | bytes 1900544 | tf_op jit(solution)/shard_map/scatter | solution.py:42
  93.2 1.7 copy.24
  94.9 15.7 %fusion = f32[256,3072]{1,0:T(8,128)} fusion(bf16[256,3072]{0,1:T(8,128)(2,1)S(1)} %scatter_custom_fusion.5, bf16[3072,3072]{1,0:T(8,128)(2,1)} %mul.31, bf16[1,1,3072,3072]{3,2,1,0:T(8,128)(2,1)} %param.13), kind=kOutput, calls=%fused_computation.13 | convolution fusion | flops 4841275392 | bytes 42467328 | tf_op jit(solution)/shard_map/dot_general | solution.py:46
  110.7 3.6 %copy.22 = f32[256,3072]{0,1:T(8,128)} copy(f32[256,3072]{1,0:T(8,128)} %fusion) | data formatting | bytes 6291456 | tf_op jit(solution)/shard_map/dot_general | solution.py:46
  114.3 2.1 scatter_custom_fusion.6
  116.4 73.5 %all-reduce.1 = bf16[256,1536]{0,1:T(8,128)(2,1)} all-reduce(f32[256,1536]{0,1:T(8,128)S(1)} %scatter_custom_fusion.6), channel_id=1, replica_groups=mesh['gx'=8,'gy'=16] {'gx','gy'}, use_global_device_ids=true, to_apply=%region_7.8 | all-reduce | flops 393216 | bytes 2359296 | tf_op jit(solution)/shard_map/psum | solution.py:60
  189.9 0.0 copy-start.1
  189.9 5.5 %fusion.33 = bf16[256,1536]{0,1:T(8,128)(2,1)} fusion(bf16[256,1536]{0,1:T(8,128)(2,1)} %all-reduce.1, bf16[1536,1536]{1,0:T(8,128)(2,1)} %param.15), kind=kOutput, calls=%fused_computation.82 | convolution fusion | flops 1207959552 | bytes 6291456 | tf_op jit(solution)/shard_map/dot_general | solution.py:61
  195.4 1.9 gather_fusion
  197.3 0.0 copy-done
  197.3 0.0 copy-done.1
  197.3 2.3 convolution_subtract_fusion
  199.6 2.2 copy.23
  201.7 0.0 copy-start.2
  201.7 8.1 %gather_fusion.1 = bf16[2560,256]{1,0:T(8,128)(2,1)} fusion(bf16[256,3072]{0,1:T(8,128)(2,1)S(1)} %copy.23, s32[3072]{0:T(1024)S(1)} %pad_clamp_fusion), kind=kCustom, calls=%fused_computation.4 | custom fusion | bytes 2631680 | tf_op jit(solution)/shard_map/gather | solution.py:67
  209.9 1.8 slice_bitcast_fusion.2
  211.7 2.6 collective-permute-start.2
  214.3 0.0 collective-permute-start.3
  214.3 0.0 copy-done.2
  214.3 2.3 multiply_reduce_fusion
  216.6 63.5 %psum.15 = f32[256]{0:T(256)S(1)} all-reduce(f32[256]{0:T(256)S(1)} %multiply_reduce_fusion), channel_id=1, replica_groups=mesh['gx'=8,'gy'=16] {'gx','gy'}, use_global_device_ids=true, to_apply=%region_9.11 | all-reduce | flops 256 | bytes 2048 | tf_op jit(solution)/shard_map/psum | solution.py:66
  280.0 0.6 broadcast_multiply_fusion
  280.6 0.0 collective-permute-done.2
  280.6 2.8 gather_fusion.2
  283.4 0.0 copy-start.3
  283.4 0.0 collective-permute-done.3
  283.4 2.8 gather_fusion.3
  286.2 0.0 copy-done.3
  286.2 0.4 fusion.9
  286.5 0.1 pad_maximum_fusion
  286.6 1.8 copy.25
  (13 shorter events, 0.1 us)
Async XLA Ops:
  0.6 196.7 %copy-start = (bf16[1,1,48,3072]{3,2,1,0:T(8,128)(2,1)S(1)}, bf16[1,1,48,3072]{3,2,1,0:T(8,128)(2,1)}, u32[]{:S(2)}) copy-start(bf16[1,1,48,3072]{3,2,1,0:T(8,128)(2,1)} %param.14) | copy-start | bytes 884740
  0.6 1.5 copy-start.5
  1.9 15.7 %copy-start.4 = (s32[1,1,2608]{2,1,0:T(1,128)S(1)}, s32[1,1,2608]{2,1,0:T(1,128)}, u32[]{:S(2)}) copy-start(s32[1,1,2608]{2,1,0:T(1,128)} %param.11) | copy-start | bytes 31300
  2.1 22.8 %copy-start.6 = (s32[1,1,16,16]{3,2,1,0:T(8,128)S(1)}, s32[1,1,16,16]{3,2,1,0:T(8,128)}, u32[]{:S(2)}) copy-start(s32[1,1,16,16]{3,2,1,0:T(8,128)} %param.12) | copy-start | bytes 3076
  7.6 72.0 %collective-permute-start = (bf16[256,640]{0,1:T(8,128)(2,1)S(1)}, bf16[256,640]{0,1:T(8,128)(2,1)S(1)}, u32[]{:S(2)}, u32[]{:S(2)}) collective-permute-start(bf16[256,640]{0,1:T(8,128)(2,1)S(1)} %scatter_custom_fusion.2), channel_id=1, source_target_pairs={{15,0},{0,1},{1,2},{2,3},{3,4},{4,5},{5,6},{6,7},{7,8},{8,9},{9,10... | collective-permute-start | bytes 983048 | tf_op jit(solution)/shard_map/ppermute | solution.py:10
  15.5 70.9 %collective-permute-start.1 = (bf16[256,640]{0,1:T(8,128)(2,1)S(1)}, bf16[256,640]{0,1:T(8,128)(2,1)}, u32[]{:S(2)}, u32[]{:S(2)}) collective-permute-start(bf16[256,640]{0,1:T(8,128)(2,1)S(1)} %scatter_custom_fusion.4), channel_id=1, source_target_pairs={{112,0},{0,16},{16,32},{32,48},{48,64},{64,80},{80,96},{96,112},{1... | collective-permute-start | bytes 983048 | tf_op jit(solution)/shard_map/ppermute | solution.py:10
  33.6 39.5 %copy-start.7 = (s32[48]{0:T(128)S(1)}, s32[48]{0:T(128)}, u32[]{:S(2)}) copy-start(s32[48]{0:T(128)} %fusion.32) | copy-start | bytes 580
  189.9 7.4 %copy-start.1 = (f32[256,3072]{1,0:T(8,128)S(1)}, f32[256,3072]{1,0:T(8,128)}, u32[]{:S(2)}) copy-start(f32[256,3072]{1,0:T(8,128)} %fusion) | copy-start | bytes 9437188
  201.7 12.6 %copy-start.2 = (bf16[256,3072]{1,0:T(8,128)(2,1)S(1)}, bf16[256,3072]{1,0:T(8,128)(2,1)}, u32[]{:S(2)}) copy-start(bf16[256,3072]{1,0:T(8,128)(2,1)} %copy.24) | copy-start | bytes 4718596
  211.7 68.9 %collective-permute-start.2 = (bf16[256,640]{0,1:T(8,128)(2,1)S(1)}, bf16[256,640]{0,1:T(8,128)(2,1)S(1)}, u32[]{:S(2)}, u32[]{:S(2)}) collective-permute-start(bf16[256,640]{0,1:T(8,128)(2,1)S(1)} %get-tuple-element.17), channel_id=1, source_target_pairs={{1,0},{2,1},{3,2},{4,3},{5,4},{6,5},{7,6},{8,7},{9,8},{10,9},{11,1... | collective-permute-start | bytes 983048 | tf_op jit(solution)/shard_map/ppermute | solution.py:10
  214.3 69.1 %collective-permute-start.3 = (bf16[256,640]{0,1:T(8,128)(2,1)}, bf16[256,640]{0,1:T(8,128)(2,1)S(1)}, u32[]{:S(2)}, u32[]{:S(2)}) collective-permute-start(bf16[256,640]{0,1:T(8,128)(2,1)} %get-tuple-element.18), channel_id=1, source_target_pairs={{16,0},{32,16},{48,32},{64,48},{80,64},{96,80},{112,96},{0,112},{1... | collective-permute-start | bytes 983048 | tf_op jit(solution)/shard_map/ppermute | solution.py:10
  283.4 2.8 copy-start.3
where the time goes:
time: 290 us; the launch traced here: 288 us
  blocking collectives  137 us (47%)
  local copies, waits for them, and re-layouts  99.7 us (34%)
  matrix products  23.5 us (8%)
  other arithmetic  20.4 us (7%)
  starting transfers between devices  6.83 us (2%)
    psum x1, blocking collectives, shards(): coarse_load = lax.psum(load_part, ('gx', 'gy'))  73.5 us
    psum x1, blocking collectives, shards(): lax.psum(jnp.sum(spread.astype(jnp.float32) * image, axis=1), ('gx', 'gy'))  63.5 us
    mul x2, local copies, waits for them, and re-layouts, shards(): tile.reshape(nblock, bsize, nblock, bsize)  47.8 us
    dot_general x1, matrix products, shards(): local_image = jnp.dot(spread, masked, preferred_element_type=jnp.float32)  15.7 us
    scatter x2, local copies, waits for them, and re-layouts, place(): return jnp.zeros_like(values).at[:, perm].set(values)  10.9 us
    gather x1, local copies, waits for them, and re-layouts, shards(): image[:, rows[:4 * faces]].astype(jnp.bfloat16).reshape(nrhs, 4, faces)  8.13 us
    scatter x1, other arithmetic, shards(): spread = spread.at[:, rows[0:faces]].set(-from_north)  6.88 us
    ppermute x4, starting transfers between devices, passed_along(): return lax.ppermute(block, axis, route)  6.83 us
  transfers between devices with their start and end apart: 4, of which 0 were waited for; matrix products, arithmetic and copies ran while one was open for 28% of the time, Pallas kernels for 0%

commit v1 on v0

v1 whole, which is shorter than its diff:
```python
import functools

import jax
import jax.numpy as jnp
from jax import lax
from jax.experimental import pallas as pl
from jax.experimental.pallas import tpu as pltpu
from jax.sharding import PartitionSpec as P

MESH = pl.DeviceIdType.MESH
BF16 = jnp.bfloat16
F32 = jnp.float32
I32 = jnp.int32
NT = (((1,), (1,)), ((), ()))


def dot(x, y):
    return jnp.dot(x, y, preferred_element_type=F32)


def dot_nt(x, y):
    return lax.dot_general(x, y, NT, preferred_element_type=F32)


def iota(shape, dim):
    return lax.broadcasted_iota(I32, shape, dim)


def unit(cond):
    return jnp.where(cond, jnp.ones((), BF16), jnp.zeros((), BF16))


def one_hot(first, count, index):
    rows = iota((count, index.shape[1]), 0).astype(jnp.int16)
    return unit(rows == (index - first).astype(jnp.int16))


def kernel(
    nx,
    ny,
    lam_hbm,
    partner_hbm,
    rows_hbm,
    mask_hbm,
    tile_hbm,
    basis_hbm,
    inverse_hbm,
    jumps_ref,
    curvature_ref,
    lam,
    partner,
    rows,
    mask,
    tile,
    basis,
    inverse,
    own,
    received,
    partner_west,
    partner_north,
    index,
    spread,
    local,
    image,
    mask_rows,
    corner_tile,
    solve,
    loads,
    parts,
    parts_in,
    face_out,
    face_in,
    face_own,
    sum_x,
    sum_y,
    local_sem,
    pair_send,
    pair_recv,
    load_send,
    load_recv,
    part_send,
    part_recv,
    sumx_send,
    sumx_recv,
    sumy_send,
    sumy_recv,
):
    a = lax.axis_index("gx")
    b = lax.axis_index("gy")
    nrhs, _, faces = lam.shape
    width = tile.shape[0]
    nblock = mask.shape[0]
    bsize = width // nblock
    group = bsize // 16
    four_cd = basis.shape[0]
    cd = four_cd // 4
    row_cd = ny * cd
    two = 2 * faces
    chunks = 4
    tall = width // chunks
    blocks = nblock // chunks
    wide = width // 3
    east = (a, lax.rem(b + 1, ny))
    west = (a, lax.rem(b + ny - 1, ny))
    south = (lax.rem(a + 1, nx), b)
    north = (lax.rem(a + nx - 1, nx), b)

    def fetch(src, dst, slot):
        copy = pltpu.make_async_copy(src, dst, local_sem.at[slot])
        copy.start()
        return copy

    lam_copy = fetch(lam_hbm, lam, 0)
    rows_copy = fetch(rows_hbm, rows, 1)
    partner_copy = fetch(partner_hbm, partner, 2)
    mask_copy = fetch(mask_hbm, mask, 3)

    def tile_copy(j):
        part = pl.ds(pl.multiple_of(j * tall, tall), tall)
        return pltpu.make_async_copy(tile_hbm.at[part], tile.at[part], local_sem.at[8 + j])

    barrier = pltpu.get_barrier_semaphore()

    @pl.loop(1, ny)
    def _(k):
        pl.semaphore_signal(barrier, inc=1, device_id=(a, lax.rem(b + k, ny)), device_id_type=MESH)

    @pl.loop(1, nx)
    def _(k):
        pl.semaphore_signal(barrier, inc=1, device_id=(lax.rem(a + k, nx), b), device_id_type=MESH)

    for j in range(chunks):
        tile_copy(j).start()
    basis_copy = fetch(basis_hbm, basis, 4)
    inverse_copies = []
    for p in range(2):
        first = pl.multiple_of(lax.rem(a + p, nx) * row_cd, 16)
        inverse_copies.append(
            fetch(inverse_hbm.at[pl.ds(first, row_cd)], inverse.at[pl.ds(p * row_cd, row_cd)], 5 + p)
        )

    lam_copy.wait()
    both = lam[...].reshape(2 * nrhs, faces)
    for f in range(2):
        pick = unit(iota((nrhs, 2 * nrhs), 1) == 2 * iota((nrhs, 2 * nrhs), 0) + f)
        own[:, f * faces : (f + 1) * faces] = dot(pick, both).astype(BF16)
    partner_copy.wait()
    pl.semaphore_wait(barrier, nx + ny - 2)

    def send(src, dst, slot, device):
        copy = pltpu.make_async_remote_copy(
            src_ref=src,
            dst_ref=dst,
            send_sem=pair_send.at[slot],
            recv_sem=pair_recv.at[slot],
            device_id=device,
            device_id_type=MESH,
        )
        copy.start()
        return copy

    east_half = pl.ds(0, faces)
    south_half = pl.ds(faces, faces)
    pairs = [
        send(partner, partner_west, 0, east),
        send(partner, partner_north, 1, south),
        send(own.at[:, east_half], received.at[:, east_half], 2, east),
        send(own.at[:, south_half], received.at[:, south_half], 3, south),
    ]

    rows_copy.wait()
    index[:, 0:faces] = rows[:, 3 * faces : 4 * faces]
    index[:, faces:two] = rows[:, faces:two]

    @pl.loop(0, 3)
    def _(j):
        n0 = pl.multiple_of(j * wide, wide)
        hot = one_hot(n0, wide, index[:, 0:two])
        spread[:, pl.ds(n0, wide)] = dot_nt(own[...], hot).astype(BF16)

    mask_copy.wait()
    inside = iota((nblock, width), 1) - bsize * iota((nblock, width), 0)
    expanded = dot(
        mask[...].astype(F32).astype(BF16), unit((inside >= 0) & (inside < bsize))
    )
    for i in range(nblock):
        mask_rows[i] = jnp.broadcast_to(expanded[i : i + 1], (16, width)).astype(BF16)

    corner_rows = rows[:, 4 * faces : 4 * faces + four_cd]
    corner_hot = one_hot(0, width, corner_rows)

    @pl.loop(0, chunks)
    def _(j):
        tile_copy(j).wait()
        part = pl.ds(pl.multiple_of(j * tall, tall), tall)
        piece = tile[part].reshape(blocks, group, 16, width)
        piece = piece * mask_rows[pl.ds(j * blocks, blocks)][:, None]
        corner_tile[part] = dot(piece.reshape(tall, width), corner_hot).astype(BF16)

    for copy in inverse_copies:
        copy.wait()
    total = inverse.shape[1]

    def over(value, count):
        return jnp.where(value >= count, value - count, value)

    def divided(value):
        return (value * (-(-(1 << 19) // cd))) >> 19

    out = iota((nx * four_cd, 1), 0)
    unit_at = divided(out)
    corner = unit_at & 3
    node = over((unit_at >> 2) + (corner >> 1), nx) * ny + over(b + (corner & 1), ny)
    column = node * cd + out - unit_at * cd
    chosen = unit(iota((nx * four_cd, total), 1) == column)
    by_row = dot_nt(chosen, inverse[...]).astype(BF16)
    load_at = iota((1, ny * four_cd), 1)
    unit_at = divided(load_at)
    corner = unit_at & 3
    source = (corner >> 1) * row_cd + over((unit_at >> 2) + (corner & 1), ny) * cd
    source = source + load_at - unit_at * cd
    widen = unit(iota((2 * row_cd, ny * four_cd), 0) == source)
    solve[...] = dot(by_row, widen).astype(BF16)

    for f, copy in enumerate(pairs[:2]):
        copy.wait()
        pair_row = (partner_west[0:1], partner_north[1:2])[f]
        face_row = (rows[:, two : 3 * faces], rows[:, 0:faces])[f]
        sub = iota((8, faces), 0)
        digits = jnp.where(sub == 0, face_row >> 8, jnp.where(sub == 1, face_row & 255, 0))
        found = dot(digits.astype(F32).astype(BF16), one_hot(0, faces, pair_row))
        index[:, two + f * faces : two + (f + 1) * faces] = (
            found[0:1] * 256.0 + found[1:2]
        ).astype(I32)
    pairs[3].wait()
    pairs[2].wait()

    @pl.loop(0, 3)
    def _(j):
        n0 = pl.multiple_of(j * wide, wide)
        hot = one_hot(n0, wide, index[:, two : 2 * two])
        at = (slice(None), pl.ds(n0, wide))
        spread[at] = (spread[at].astype(F32) - dot_nt(received[...], hot)).astype(BF16)

    corner_load = dot(spread[...], corner_tile[...]).astype(BF16)
    same = unit(iota((four_cd, four_cd), 0) == iota((four_cd, four_cd), 1))
    mine = pl.ds(pl.multiple_of(b * four_cd, 16), four_cd)
    loads[mine] = dot_nt(same, corner_load).astype(BF16)

    def load_copy(k):
        return pltpu.make_async_remote_copy(
            src_ref=loads.at[mine],
            dst_ref=loads.at[mine],
            send_sem=load_send.at[k],
            recv_sem=load_recv.at[k],
            device_id=(a, lax.rem(b + k, ny)),
            device_id_type=MESH,
        )

    pl.loop(1, ny)(lambda k: load_copy(k).start())

    @pl.loop(0, 3)
    def _(j):
        at = (slice(None), pl.ds(pl.multiple_of(j * wide, wide), wide))
        masked = tile[at].reshape(nblock, group, 16, wide) * mask_rows[:, :, at[1]][:, None]
        local[at] = dot(spread[...], masked.reshape(width, wide))

    pl.loop(1, ny)(lambda k: load_copy(k).wait())

    parts[...] = dot(solve[...], loads[...]).astype(BF16)

    def part_copy(k):
        to = lax.rem(a + k, nx)
        return pltpu.make_async_remote_copy(
            src_ref=parts.at[pl.ds(pl.multiple_of(to * four_cd, 16), four_cd)],
            dst_ref=parts_in.at[k],
            send_sem=part_send.at[k],
            recv_sem=part_recv.at[k],
            device_id=(to, b),
            device_id_type=MESH,
        )

    pl.loop(1, nx)(lambda k: part_copy(k).start())
    basis_copy.wait()
    corners = parts[pl.ds(pl.multiple_of(a * four_cd, 16), four_cd)].astype(F32)
    for k in range(1, nx):
        part_copy(k).wait()
        corners = corners + parts_in[k].astype(F32)
    corners = corners.T.astype(BF16)

    product = jnp.zeros((nrhs, 128), F32)
    for j in range(3):
        at = (slice(None), slice(j * wide, (j + 1) * wide))
        full = local[at] - dot(corners, basis[at])
        image[at] = full.astype(BF16)
        full = full * spread[at].astype(F32)
        for q in range(wide // 128):
            product = product + full[:, q * 128 : (q + 1) * 128]
    mine_x = pl.ds(pl.multiple_of(a * 8, 8), 8)
    sum_x[mine_x] = lax.dot_general(
        jnp.ones((8, 128), F32), product, NT, precision=lax.Precision.HIGHEST, preferred_element_type=F32
    )

    def sumx_copy(k):
        return pltpu.make_async_remote_copy(
            src_ref=sum_x.at[mine_x],
            dst_ref=sum_x.at[mine_x],
            send_sem=sumx_send.at[k],
            recv_sem=sumx_recv.at[k],
            device_id=(lax.rem(a + k, nx), b),
            device_id_type=MESH,
        )

    pl.loop(1, nx)(lambda k: sumx_copy(k).start())

    def gathered(first, count):
        return dot(image[...], one_hot(0, width, index[:, first : first + count])).astype(BF16)

    face_out[:, 0:faces] = gathered(two, faces)
    pairs.append(send(face_out.at[:, east_half], face_in.at[:, east_half], 4, west))
    face_out[:, faces:two] = gathered(two + faces, faces)
    pairs.append(send(face_out.at[:, south_half], face_in.at[:, south_half], 5, north))

    pl.loop(1, nx)(lambda k: sumx_copy(k).wait())
    mine_y = pl.ds(pl.multiple_of(b * 8, 8), 8)
    sum_y[mine_y] = jnp.sum(sum_x[...].reshape(nx, 8, nrhs), axis=0)

    def sumy_copy(k):
        return pltpu.make_async_remote_copy(
            src_ref=sum_y.at[mine_y],
            dst_ref=sum_y.at[mine_y],
            send_sem=sumy_send.at[k],
            recv_sem=sumy_recv.at[k],
            device_id=(a, lax.rem(b + k, ny)),
            device_id_type=MESH,
        )

    pl.loop(1, ny)(lambda k: sumy_copy(k).start())
    face_own[...] = gathered(0, two)
    pl.loop(1, ny)(lambda k: sumy_copy(k).wait())
    everything = jnp.sum(sum_y[...].reshape(ny, 8, nrhs), axis=0)
    curvature_ref[...] = everything[0:1] / (2.0 * faces * nx * ny)

    pairs[5].wait()
    pairs[4].wait()
    jump = (face_own[...].astype(F32) - face_in[...].astype(F32)).astype(BF16)
    mixed = jnp.zeros((2 * nrhs, faces), F32)
    for f in range(2):
        lay = unit(iota((2 * nrhs, nrhs), 0) == 2 * iota((2 * nrhs, nrhs), 1) + f)
        mixed = mixed + dot(lay, jump[:, f * faces : (f + 1) * faces])
    jumps_ref[...] = mixed.astype(BF16).reshape(nrhs, 2, faces)


def shards(multipliers, partner, interface_rows, block_mask, tiles, basis, coarse_inverse):
    nx = lax.axis_size("gx")
    ny = lax.axis_size("gy")
    lam = multipliers[0, 0]
    nrhs, _, faces = lam.shape
    rows = interface_rows[0]
    width = tiles.shape[2]
    nblock = block_mask.shape[2]
    four_cd = basis.shape[2]
    total = coarse_inverse.shape[1]
    row_cd = total // nx
    dma = pltpu.SemaphoreType.DMA
    vmem = pltpu.VMEM
    two = 2 * faces
    jumps, curvature = pl.pallas_call(
        functools.partial(kernel, nx, ny),
        out_shape=(
            jax.ShapeDtypeStruct(lam.shape, BF16),
            jax.ShapeDtypeStruct((1, nrhs), F32),
        ),
        in_specs=[pl.BlockSpec(memory_space=pl.ANY)] * 7,
        out_specs=(pl.BlockSpec(memory_space=vmem), pl.BlockSpec(memory_space=vmem)),
        scratch_shapes=[
            vmem(lam.shape, BF16),
            vmem((2, faces), I32),
            vmem(rows.shape, I32),
            vmem((nblock, nblock), I32),
            vmem((width, width), BF16),
            vmem((four_cd, width), BF16),
            vmem((2 * row_cd, total), BF16),
            vmem((nrhs, two), BF16),
            vmem((nrhs, two), BF16),
            vmem((2, faces), I32),
            vmem((2, faces), I32),
            vmem((1, 2 * two), I32),
            vmem((nrhs, width), BF16),
            vmem((nrhs, width), F32),
            vmem((nrhs, width), BF16),
            vmem((nblock, 16, width), BF16),
            vmem((width, four_cd), BF16),
            vmem((nx * four_cd, ny * four_cd), BF16),
            vmem((ny * four_cd, nrhs), BF16),
            vmem((nx * four_cd, nrhs), BF16),
            vmem((nx, four_cd, nrhs), BF16),
            vmem((nrhs, two), BF16),
            vmem((nrhs, two), BF16),
            vmem((nrhs, two), BF16),
            vmem((nx * 8, nrhs), F32),
            vmem((ny * 8, nrhs), F32),
            dma((12,)),
            dma((6,)),
            dma((6,)),
            dma((ny,)),
            dma((ny,)),
            dma((nx,)),
            dma((nx,)),
            dma((nx,)),
            dma((nx,)),
            dma((ny,)),
            dma((ny,)),
        ],
        compiler_params=pltpu.CompilerParams(
            collective_id=0, has_side_effects=True, vmem_limit_bytes=60 * 2**20
        ),
    )(lam, partner[0, 0], rows, block_mask[0, 0], tiles[0, 0], basis[0, 0], coarse_inverse)
    return jumps[None, None], curvature.reshape(nrhs)


def solution(mesh):
    in_specs = (
        P("gx", "gy", None, None, None),
        P("gx", "gy", None, None),
        P("gx", "gy", None),
        P("gx", "gy", None, None),
        P("gx", "gy", None, None),
        P("gx", "gy", None, None),
        P(),
    )
    out_specs = (P("gx", "gy", None, None, None), P())
    return jax.shard_map(shards, mesh=mesh, in_specs=in_specs, out_specs=out_specs, check_vma=False)
```

time: 290 us -> 54.7 us (0.19)
  the two profiles are of different devices: /device:TPU:1 before, /device:TPU:8 now
where the time goes in v1:
time: 54.7 us; the launch traced here: 54.5 us
  Pallas kernels  50.2 us (92%)
  local copies, waits for them, and re-layouts  3.59 us (7%)
  between operations  0.64 us (1%)
    pallas_call x1, Pallas kernels, shards(): pl.pallas_call(functools.partial(kernel, nx, ny), out_shape=(jax.ShapeDty...  50.2 us
    unnamed x2, local copies, waits for them, and re-layouts  3.59 us

profile of v1, /device:TPU:8, one launch (start us, length us, event | category | flops | bytes accessed | tf_op | source)
XLA Modules:
  0.0 54.5 jit_solution(11103986375634902377)
XLA Ops:
  0.6 50.2 %shard_map.86 = (bf16[256,2,640]{2,1,0:T(2,128)(2,1)}, f32[1,256]{1,0:T(1,128)}) custom-call(bf16[256,2,640]{2,1,0:T(2,128)(2,1)} %bitcast.9, s32[2,640]{1,0:T(2,128)} %bitcast.14, s32[1,2608]{1,0:T(1,128)} %bitcast.12, s32[16,16]{1,0:T(8,128)} %bitcast.13, bf16[3072,3072]{1,0:T(8,128)(2,1)} %bitcast.8, bf16[48,3072]{1,0:T(8,128)(2,1)} %bitcast.11, ...), custom_call_target="tpu_custom_call" | custom-call | tf_op jit(solution)/shard_map/pallas_call | solution.py:368
  50.9 2.4 %copy.11 = bf16[1,1,256,2,640]{4,3,2,1,0:T(2,128)(2,1)} copy(bf16[1,1,256,2,640]{4,3,2,1,0:T(2,128)(2,1)} %bitcast.10) | data formatting | bytes 1310720
  53.3 1.2 %copy.12 = f32[256]{0:T(256)} copy(f32[256]{0:T(256)} %bitcast.15) | data formatting | bytes 2048

commit v2 on v1

v2 whole, which is shorter than its diff:
```python
import functools

import jax
import jax.numpy as jnp
from jax import lax
from jax.experimental import pallas as pl
from jax.experimental.pallas import tpu as pltpu
from jax.sharding import PartitionSpec as P

MESH = pl.DeviceIdType.MESH
BF16 = jnp.bfloat16
F32 = jnp.float32
I32 = jnp.int32
NT = (((1,), (1,)), ((), ()))


def dot(x, y):
    return jnp.dot(x, y, preferred_element_type=F32)


def dot_nt(x, y):
    return lax.dot_general(x, y, NT, preferred_element_type=F32)


def iota(shape, dim):
    return lax.broadcasted_iota(I32, shape, dim)


def unit(cond):
    return jnp.where(cond, jnp.ones((), BF16), jnp.zeros((), BF16))


def one_hot(first, count, index):
    rows = iota((count, index.shape[1]), 0).astype(jnp.int16)
    return unit(rows == (index - first).astype(jnp.int16))


def kernel(
    nx,
    ny,
    lam_hbm,
    partner_hbm,
    rows_hbm,
    mask_hbm,
    tile_hbm,
    basis_hbm,
    inverse_hbm,
    jump_ref,
    curvature_ref,
    lam,
    partner,
    rows,
    mask,
    tile,
    joint,
    inverse,
    own,
    received,
    partner_west,
    partner_north,
    index,
    spread,
    product,
    image,
    mask_rows,
    solve,
    loads,
    bilinear,
    stack,
    basis_out,
    parts,
    parts_in,
    face_out,
    face_in,
    face_own,
    sum_x,
    sum_y,
    local_sem,
    pair_send,
    pair_recv,
    load_send,
    load_recv,
    bil_send,
    bil_recv,
    part_send,
    part_recv,
    sumx_send,
    sumx_recv,
    sumy_send,
    sumy_recv,
):
    a = lax.axis_index("gx")
    b = lax.axis_index("gy")
    nrhs, _, faces = lam.shape
    width = tile.shape[0]
    nblock = mask.shape[0]
    bsize = width // nblock
    group = bsize // 16
    four_cd = basis_hbm.shape[0]
    cd = four_cd // 4
    row_cd = ny * cd
    two = 2 * faces
    chunks = 4
    tall = width // chunks
    blocks = nblock // chunks
    wide = width // 3
    east = (a, lax.rem(b + 1, ny))
    west = (a, lax.rem(b + ny - 1, ny))
    south = (lax.rem(a + 1, nx), b)
    north = (lax.rem(a + nx - 1, nx), b)

    def fetch(src, dst, slot):
        copy = pltpu.make_async_copy(src, dst, local_sem.at[slot])
        copy.start()
        return copy

    half = nrhs // 2
    lam_copies = [
        fetch(lam_hbm.at[pl.ds(h * half, half)], lam.at[pl.ds(h * half, half)], (0, 7)[h]) for h in range(2)
    ]
    rows_copy = fetch(rows_hbm, rows, 1)
    partner_copy = fetch(partner_hbm, partner, 2)
    mask_copy = fetch(mask_hbm, mask, 3)

    def tile_copy(j):
        part = pl.ds(pl.multiple_of(j * tall, tall), tall)
        return pltpu.make_async_copy(tile_hbm.at[part], tile.at[part], local_sem.at[8 + j])

    barrier = pltpu.get_barrier_semaphore()

    @pl.loop(1, ny)
    def _(k):
        pl.semaphore_signal(barrier, inc=1, device_id=(a, lax.rem(b + k, ny)), device_id_type=MESH)

    @pl.loop(1, nx)
    def _(k):
        pl.semaphore_signal(barrier, inc=1, device_id=(lax.rem(a + k, nx), b), device_id_type=MESH)

    for j in range(chunks):
        tile_copy(j).start()
    basis_rows = pl.ds(nrhs, four_cd)
    basis_copies = [
        fetch(basis_hbm, joint.at[pl.ds(four_cd, four_cd)], 4),
        fetch(basis_hbm, image.at[basis_rows], 12),
    ]
    inverse_copies = []
    for p in range(2):
        first = pl.multiple_of(lax.rem(a + p, nx) * row_cd, 16)
        inverse_copies.append(
            fetch(inverse_hbm.at[pl.ds(first, row_cd)], inverse.at[pl.ds(p * row_cd, row_cd)], 5 + p)
        )

    def send(src, dst, slot, device):
        copy = pltpu.make_async_remote_copy(
            src_ref=src,
            dst_ref=dst,
            send_sem=pair_send.at[slot],
            recv_sem=pair_recv.at[slot],
            device_id=device,
            device_id_type=MESH,
        )
        copy.start()
        return copy

    east_half = pl.ds(0, faces)
    south_half = pl.ds(faces, faces)
    at_row, at_column = iota((nrhs, nrhs), 0), iota((nrhs, nrhs), 1)
    pick = unit(at_column == jnp.where(at_row < half, 2 * at_row, 2 * (at_row - half) + 1))
    pairs = []
    for h in range(2):
        part = pl.ds(h * half, half)
        lam_copies[h].wait()
        apart = dot(pick, lam[part].reshape(nrhs, faces)).astype(BF16)
        own[part, 0:faces] = apart[:half]
        own[part, faces:two] = apart[half:]
        if h == 0:
            partner_copy.wait()
            pl.semaphore_wait(barrier, nx + ny - 2)
            pairs.append(send(partner, partner_west, 0, east))
            pairs.append(send(partner, partner_north, 1, south))
        pairs.append(send(own.at[part, east_half], received.at[part, east_half], 2 + h, east))
        pairs.append(send(own.at[part, south_half], received.at[part, south_half], 4 + h, south))

    rows_copy.wait()
    index[:, 0:faces] = rows[:, 3 * faces : 4 * faces]
    index[:, faces:two] = rows[:, faces:two]

    @pl.loop(0, 3)
    def _(j):
        n0 = pl.multiple_of(j * wide, wide)
        hot = one_hot(n0, wide, index[:, 0:two])
        spread[:, pl.ds(n0, wide)] = dot_nt(own[...], hot).astype(BF16)

    mask_copy.wait()
    inside = iota((nblock, width), 1) - bsize * iota((nblock, width), 0)
    expanded = dot(
        mask[...].astype(F32).astype(BF16), unit((inside >= 0) & (inside < bsize))
    )
    for i in range(nblock):
        mask_rows[i] = jnp.broadcast_to(expanded[i : i + 1], (16, width)).astype(BF16)

    corner_rows = rows[:, 4 * faces : 4 * faces + four_cd]
    corner_hot = one_hot(0, width, corner_rows)

    @pl.loop(0, chunks)
    def _(j):
        tile_copy(j).wait()
        part = pl.ds(pl.multiple_of(j * tall, tall), tall)
        piece = tile[part].reshape(blocks, group, 16, width)
        piece = piece * mask_rows[pl.ds(j * blocks, blocks)][:, None]
        joint[0:four_cd, part] = dot(piece.reshape(tall, width), corner_hot).T.astype(BF16)

    for f, copy in enumerate(pairs[:2]):
        copy.wait()
        pair_row = (partner_west[0:1], partner_north[1:2])[f]
        face_row = (rows[:, two : 3 * faces], rows[:, 0:faces])[f]
        sub = iota((8, faces), 0)
        digits = jnp.where(sub == 0, face_row >> 8, jnp.where(sub == 1, face_row & 255, 0))
        found = dot(digits.astype(F32).astype(BF16), one_hot(0, faces, pair_row))
        index[:, two + f * faces : two + (f + 1) * faces] = (
            found[0:1] * 256.0 + found[1:2]
        ).astype(I32)
    for copy in pairs[2:6]:
        copy.wait()

    @pl.loop(0, 3)
    def _(j):
        n0 = pl.multiple_of(j * wide, wide)
        hot = one_hot(n0, wide, index[:, two : 2 * two])
        at = (slice(None), pl.ds(n0, wide))
        spread[at] = (spread[at].astype(F32) - dot_nt(received[...], hot)).astype(BF16)

    for copy in basis_copies:
        copy.wait()
    products = dot_nt(joint[...], spread[...]).astype(BF16)
    mine = pl.ds(pl.multiple_of(b * four_cd, 16), four_cd)
    loads[mine] = products[:four_cd]

    def load_copy(k):
        return pltpu.make_async_remote_copy(
            src_ref=loads.at[mine],
            dst_ref=loads.at[mine],
            send_sem=load_send.at[k],
            recv_sem=load_recv.at[k],
            device_id=(a, lax.rem(b + k, ny)),
            device_id_type=MESH,
        )

    pl.loop(1, ny)(lambda k: load_copy(k).start())

    mine_a = pl.ds(pl.multiple_of(a * four_cd, 16), four_cd)
    bilinear[mine_a] = products[four_cd:]

    def bil_copy(k):
        return pltpu.make_async_remote_copy(
            src_ref=bilinear.at[mine_a],
            dst_ref=bilinear.at[mine_a],
            send_sem=bil_send.at[k],
            recv_sem=bil_recv.at[k],
            device_id=(lax.rem(a + k, nx), b),
            device_id_type=MESH,
        )

    pl.loop(1, nx)(lambda k: bil_copy(k).start())

    product[...] = jnp.zeros_like(product)

    @pl.loop(0, 3)
    def _(j):
        at = (slice(None), pl.ds(pl.multiple_of(j * wide, wide), wide))
        masked = tile[at].reshape(nblock, group, 16, wide) * mask_rows[:, :, at[1]][:, None]
        full = dot(spread[...], masked.reshape(width, wide))
        image[0:nrhs, at[1]] = full.astype(BF16)
        full = full * spread[at].astype(F32)
        total = product[...]
        for q in range(wide // 128):
            total = total + full[:, q * 128 : (q + 1) * 128]
        product[...] = total

    def gathered(first, count):
        both = dot(image[...], one_hot(0, width, index[:, first : first + count])).astype(BF16)
        return both[:nrhs], both[nrhs:]

    face_out[:, 0:faces], basis_out[:, 0:faces] = gathered(two, faces)
    pairs.append(send(face_out.at[:, east_half], face_in.at[:, east_half], 6, west))

    for copy in inverse_copies:
        copy.wait()
    total = inverse.shape[1]

    def over(value, count):
        return jnp.where(value >= count, value - count, value)

    def divided(value):
        return (value * (-(-(1 << 19) // cd))) >> 19

    load_at = iota((1, ny * four_cd), 1)
    unit_at = divided(load_at)
    corner = unit_at & 3
    source = (corner >> 1) * row_cd + over((unit_at >> 2) + (corner & 1), ny) * cd
    source = source + load_at - unit_at * cd
    widen = unit(iota((2 * row_cd, ny * four_cd), 0) == source)
    nodes_cd = 8 * cd
    out = iota((nx * nodes_cd, 1), 0)
    unit_at = divided(out)
    place = unit_at & 7
    down = jnp.where(place < 4, place >> 1, jnp.where(place < 6, place - 4, 2))
    along = jnp.where(place < 4, place & 1, jnp.where(place < 6, 2, place - 6))
    node = over((unit_at >> 3) + down, nx) * ny + over(b + along, ny)
    column = node * cd + out - unit_at * cd
    chosen = unit(iota((nx * nodes_cd, total), 1) == column)
    solve[...] = dot(dot_nt(chosen, inverse[...]).astype(BF16), widen).astype(BF16)

    pl.loop(1, ny)(lambda k: load_copy(k).wait())
    solution_part = dot(solve[...], loads[...])
    parts[...] = solution_part.astype(BF16)

    def part_copy(k):
        to = lax.rem(a + k, nx)
        return pltpu.make_async_remote_copy(
            src_ref=parts.at[pl.ds(pl.multiple_of(to * nodes_cd, 16), nodes_cd)],
            dst_ref=parts_in.at[k],
            send_sem=part_send.at[k],
            recv_sem=part_recv.at[k],
            device_id=(to, b),
            device_id_type=MESH,
        )

    pl.loop(1, nx)(lambda k: part_copy(k).start())

    pl.loop(1, nx)(lambda k: bil_copy(k).wait())
    at_corners = solution_part.reshape(nx, nodes_cd, nrhs)[:, :four_cd].reshape(nx * four_cd, nrhs)
    coarse = jnp.sum(at_corners * bilinear[...].astype(F32), axis=0, keepdims=True)
    fine = lax.dot_general(
        jnp.ones((8, 128), F32), product[...], NT, precision=lax.Precision.HIGHEST, preferred_element_type=F32
    )
    mine_y = pl.ds(pl.multiple_of(b * 8, 8), 8)
    sum_y[mine_y] = fine - coarse

    def sumy_copy(k):
        return pltpu.make_async_remote_copy(
            src_ref=sum_y.at[mine_y],
            dst_ref=sum_y.at[mine_y],
            send_sem=sumy_send.at[k],
            recv_sem=sumy_recv.at[k],
            device_id=(a, lax.rem(b + k, ny)),
            device_id_type=MESH,
        )

    pl.loop(1, ny)(lambda k: sumy_copy(k).start())

    face_out[:, faces:two], basis_out[:, faces:two] = gathered(two + faces, faces)
    pairs.append(send(face_out.at[:, south_half], face_in.at[:, south_half], 7, north))
    theirs = pl.ds(four_cd, four_cd)
    pairs.append(send(basis_out.at[:, east_half], stack.at[theirs, east_half], 8, west))
    pairs.append(send(basis_out.at[:, south_half], stack.at[theirs, south_half], 9, north))
    face_own[...], stack[0:four_cd] = gathered(0, two)
    pl.loop(1, ny)(lambda k: sumy_copy(k).wait())
    mine_x = pl.ds(pl.multiple_of(a * 8, 8), 8)
    sum_x[mine_x] = jnp.sum(sum_y[...].reshape(ny, 8, nrhs), axis=0)

    def sumx_copy(k):
        return pltpu.make_async_remote_copy(
            src_ref=sum_x.at[mine_x],
            dst_ref=sum_x.at[mine_x],
            send_sem=sumx_send.at[k],
            recv_sem=sumx_recv.at[k],
            device_id=(lax.rem(a + k, nx), b),
            device_id_type=MESH,
        )

    pl.loop(1, nx)(lambda k: sumx_copy(k).start())

    nodes = parts[pl.ds(pl.multiple_of(a * nodes_cd, 16), nodes_cd)].astype(F32)
    for k in range(1, nx):
        part_copy(k).wait()
        nodes = nodes + parts_in[k].astype(F32)
    nodes = nodes.T.astype(BF16)
    pairs[8].wait()
    pairs[9].wait()
    corrections = []
    for f in range(2):
        row = iota((nodes_cd, 1), 0)
        unit_at = divided(row)
        corner = unit_at & 3
        beyond = (
            jnp.where(corner & 1 == 0, 1 + corner, 4 + (corner >> 1)),
            jnp.where(corner < 2, 2 + corner, 4 + corner),
        )[f]
        place = jnp.where(unit_at < 4, corner, beyond)
        hit = iota((nodes_cd, nodes_cd), 1) == place * cd + row - unit_at * cd
        pick = jnp.where(row < four_cd, 1.0, -1.0) * jnp.where(hit, 1.0, 0.0)
        coefficient = dot_nt(nodes, pick.astype(BF16)).astype(BF16)
        corrections.append(dot(coefficient, stack[:, f * faces : (f + 1) * faces]))

    pl.loop(1, nx)(lambda k: sumx_copy(k).wait())
    everything = jnp.sum(sum_x[...].reshape(nx, 8, nrhs), axis=0)
    curvature_ref[...] = everything[0:1] / (2.0 * faces * nx * ny)

    pairs[7].wait()
    pairs[6].wait()
    for f in range(2):
        at = (slice(None), slice(f * faces, (f + 1) * faces))
        jump = face_own[at].astype(F32) - face_in[at].astype(F32) - corrections[f]
        jump_ref[at] = jump.astype(BF16)


def finish(jump, curvature, jumps_ref, curvature_ref):
    nrhs = jump.shape[0]
    faces = jump.shape[1] // 2
    half = nrhs // 2
    at_row, at_column = iota((nrhs, nrhs), 0), iota((nrhs, nrhs), 1)
    lay = unit(at_row == jnp.where(at_column < half, 2 * at_column, 2 * (at_column - half) + 1))
    for h in range(2):
        part = slice(h * half, (h + 1) * half)
        apart = jnp.concatenate([jump[part, :faces], jump[part, faces:]], axis=0)
        jumps_ref[part] = dot(lay, apart).astype(BF16).reshape(half, 2, faces)
    curvature_ref[...] = curvature[...]


def shards(multipliers, partner, interface_rows, block_mask, tiles, basis, coarse_inverse):
    nx = lax.axis_size("gx")
    ny = lax.axis_size("gy")
    lam = multipliers[0, 0]
    nrhs, _, faces = lam.shape
    rows = interface_rows[0]
    width = tiles.shape[2]
    nblock = block_mask.shape[2]
    four_cd = basis.shape[2]
    total = coarse_inverse.shape[1]
    row_cd = total // nx
    dma = pltpu.SemaphoreType.DMA
    vmem = pltpu.VMEM
    two = 2 * faces
    jump, curvature = pl.pallas_call(
        functools.partial(kernel, nx, ny),
        out_shape=(
            jax.ShapeDtypeStruct((nrhs, two), BF16),
            jax.ShapeDtypeStruct((1, nrhs), F32),
        ),
        in_specs=[pl.BlockSpec(memory_space=pl.ANY)] * 7,
        out_specs=(pl.BlockSpec(memory_space=vmem), pl.BlockSpec(memory_space=vmem)),
        scratch_shapes=[
            vmem(lam.shape, BF16),
            vmem((2, faces), I32),
            vmem(rows.shape, I32),
            vmem((nblock, nblock), I32),
            vmem((width, width), BF16),
            vmem((2 * four_cd, width), BF16),
            vmem((2 * row_cd, total), BF16),
            vmem((nrhs, two), BF16),
            vmem((nrhs, two), BF16),
            vmem((2, faces), I32),
            vmem((2, faces), I32),
            vmem((1, 2 * two), I32),
            vmem((nrhs, width), BF16),
            vmem((nrhs, 128), F32),
            vmem((nrhs + four_cd, width), BF16),
            vmem((nblock, 16, width), BF16),
            vmem((2 * nx * four_cd, ny * four_cd), BF16),
            vmem((ny * four_cd, nrhs), BF16),
            vmem((nx * four_cd, nrhs), BF16),
            vmem((2 * four_cd, two), BF16),
            vmem((four_cd, two), BF16),
            vmem((2 * nx * four_cd, nrhs), BF16),
            vmem((nx, 2 * four_cd, nrhs), BF16),
            vmem((nrhs, two), BF16),
            vmem((nrhs, two), BF16),
            vmem((nrhs, two), BF16),
            vmem((nx * 8, nrhs), F32),
            vmem((ny * 8, nrhs), F32),
            dma((13,)),
            dma((10,)),
            dma((10,)),
            dma((ny,)),
            dma((ny,)),
            dma((nx,)),
            dma((nx,)),
            dma((nx,)),
            dma((nx,)),
            dma((nx,)),
            dma((nx,)),
            dma((ny,)),
            dma((ny,)),
        ],
        compiler_params=pltpu.CompilerParams(
            collective_id=0, has_side_effects=True, vmem_limit_bytes=60 * 2**20
        ),
    )(lam, partner[0, 0], rows, block_mask[0, 0], tiles[0, 0], basis[0, 0], coarse_inverse)
    jumps, curvature = pl.pallas_call(
        finish,
        out_shape=(jax.ShapeDtypeStruct(lam.shape, BF16), jax.ShapeDtypeStruct((1, nrhs), F32)),
        in_specs=[pl.BlockSpec(memory_space=vmem)] * 2,
        out_specs=(pl.BlockSpec(memory_space=vmem), pl.BlockSpec(memory_space=vmem)),
    )(jump, curvature)
    return jumps[None, None], curvature.reshape(nrhs)


def solution(mesh):
    in_specs = (
        P("gx", "gy", None, None, None),
        P("gx", "gy", None, None),
        P("gx", "gy", None),
        P("gx", "gy", None, None),
        P("gx", "gy", None, None),
        P("gx", "gy", None, None),
        P(),
    )
    out_specs = (P("gx", "gy", None, None, None), P())
    return jax.shard_map(shards, mesh=mesh, in_specs=in_specs, out_specs=out_specs, check_vma=False)
```

time: 54.7 us -> 50.1 us (0.916)
  the two profiles are of different devices: /device:TPU:8 before, /device:TPU:1 now
where the time goes in v2:
time: 50.1 us; the launch traced here: 49.9 us
  Pallas kernels  49.3 us (98%)
  between operations  0.64 us (1%)
    pallas_call x1, Pallas kernels, shards(): pl.pallas_call(functools.partial(kernel, nx, ny), out_shape=(jax.ShapeDty...  47 us
    pallas_call x1, Pallas kernels, shards(): pl.pallas_call(finish, out_shape=(jax.ShapeDtypeStruct(lam.shape, BF16),...  2.32 us

profile of v2, /device:TPU:1, one launch (start us, length us, event | category | flops | bytes accessed | tf_op | source)
XLA Modules:
  0.0 49.9 jit_solution(12182007080663290419)
XLA Ops:
  0.6 47.0 %shard_map.86 = (bf16[256,1280]{1,0:T(8,128)(2,1)}, f32[1,256]{1,0:T(1,128)}) custom-call(bf16[256,2,640]{2,1,0:T(2,128)(2,1)} %bitcast.9, s32[2,640]{1,0:T(2,128)} %bitcast.13, s32[1,2608]{1,0:T(1,128)} %bitcast.11, s32[16,16]{1,0:T(8,128)} %bitcast.12, bf16[3072,3072]{1,0:T(8,128)(2,1)} %bitcast.8, bf16[48,3072]{1,0:T(8,128)(2,1)} %bitcast.10, ...), custom_call_target="tpu_custom_call" | custom-call | tf_op jit(solution)/shard_map/pallas_call | solution.py:435
  47.6 2.3 %shard_map.87 = (bf16[256,2,640]{2,1,0:T(2,128)(2,1)}, f32[1,256]{1,0:T(1,128)}) custom-call(bf16[256,1280]{1,0:T(8,128)(2,1)} %get-tuple-element.6.jump, f32[1,256]{1,0:T(1,128)} %get-tuple-element.7.curvature), custom_call_target="tpu_custom_call" | custom-call | tf_op jit(solution)/shard_map/pallas_call | solution.py:490

commit v3 on v2

--- a/solution.py
+++ b/solution.py
@@ -100,6 +100,7 @@
     cd = four_cd // 4
     row_cd = ny * cd
     two = 2 * faces
+    first_piece = faces * 2 // 5 // 128 * 128
     chunks = 4
     tall = width // chunks
     blocks = nblock // chunks
@@ -210,80 +211,6 @@
         piece = piece * mask_rows[pl.ds(j * blocks, blocks)][:, None]
         joint[0:four_cd, part] = dot(piece.reshape(tall, width), corner_hot).T.astype(BF16)
 
-    for f, copy in enumerate(pairs[:2]):
-        copy.wait()
-        pair_row = (partner_west[0:1], partner_north[1:2])[f]
-        face_row = (rows[:, two : 3 * faces], rows[:, 0:faces])[f]
-        sub = iota((8, faces), 0)
-        digits = jnp.where(sub == 0, face_row >> 8, jnp.where(sub == 1, face_row & 255, 0))
-        found = dot(digits.astype(F32).astype(BF16), one_hot(0, faces, pair_row))
-        index[:, two + f * faces : two + (f + 1) * faces] = (
-            found[0:1] * 256.0 + found[1:2]
-        ).astype(I32)
-    for copy in pairs[2:6]:
-        copy.wait()
-
-    @pl.loop(0, 3)
-    def _(j):
-        n0 = pl.multiple_of(j * wide, wide)
-        hot = one_hot(n0, wide, index[:, two : 2 * two])
-        at = (slice(None), pl.ds(n0, wide))
-        spread[at] = (spread[at].astype(F32) - dot_nt(received[...], hot)).astype(BF16)
-
-    for copy in basis_copies:
-        copy.wait()
-    products = dot_nt(joint[...], spread[...]).astype(BF16)
-    mine = pl.ds(pl.multiple_of(b * four_cd, 16), four_cd)
-    loads[mine] = products[:four_cd]
-
-    def load_copy(k):
-        return pltpu.make_async_remote_copy(
-            src_ref=loads.at[mine],
-            dst_ref=loads.at[mine],
-            send_sem=load_send.at[k],
-            recv_sem=load_recv.at[k],
-            device_id=(a, lax.rem(b + k, ny)),
-            device_id_type=MESH,
-        )
-
-    pl.loop(1, ny)(lambda k: load_copy(k).start())
-
-    mine_a = pl.ds(pl.multiple_of(a * four_cd, 16), four_cd)
-    bilinear[mine_a] = products[four_cd:]
-
-    def bil_copy(k):
-        return pltpu.make_async_remote_copy(
-            src_ref=bilinear.at[mine_a],
-            dst_ref=bilinear.at[mine_a],
-            send_sem=bil_send.at[k],
-            recv_sem=bil_recv.at[k],
-            device_id=(lax.rem(a + k, nx), b),
-            device_id_type=MESH,
-        )
-
-    pl.loop(1, nx)(lambda k: bil_copy(k).start())
-
-    product[...] = jnp.zeros_like(product)
-
-    @pl.loop(0, 3)
-    def _(j):
-        at = (slice(None), pl.ds(pl.multiple_of(j * wide, wide), wide))
-        masked = tile[at].reshape(nblock, group, 16, wide) * mask_rows[:, :, at[1]][:, None]
-        full = dot(spread[...], masked.reshape(width, wide))
-        image[0:nrhs, at[1]] = full.astype(BF16)
-        full = full * spread[at].astype(F32)
-        total = product[...]
-        for q in range(wide // 128):
-            total = total + full[:, q * 128 : (q + 1) * 128]
-        product[...] = total
-
-    def gathered(first, count):
-        both = dot(image[...], one_hot(0, width, index[:, first : first + count])).astype(BF16)
-        return both[:nrhs], both[nrhs:]
-
-    face_out[:, 0:faces], basis_out[:, 0:faces] = gathered(two, faces)
-    pairs.append(send(face_out.at[:, east_half], face_in.at[:, east_half], 6, west))
-
     for copy in inverse_copies:
         copy.wait()
     total = inverse.shape[1]
@@ -311,6 +238,73 @@
     chosen = unit(iota((nx * nodes_cd, total), 1) == column)
     solve[...] = dot(dot_nt(chosen, inverse[...]).astype(BF16), widen).astype(BF16)
 
+    for f, copy in enumerate(pairs[:2]):
+        copy.wait()
+        pair_row = (partner_west[0:1], partner_north[1:2])[f]
+        face_row = (rows[:, two : 3 * faces], rows[:, 0:faces])[f]
+        sub = iota((8, faces), 0)
+        digits = jnp.where(sub == 0, face_row >> 8, jnp.where(sub == 1, face_row & 255, 0))
+        found = dot(digits.astype(F32).astype(BF16), one_hot(0, faces, pair_row))
+        index[:, two + f * faces : two + (f + 1) * faces] = (
+            found[0:1] * 256.0 + found[1:2]
+        ).astype(I32)
+    for copy in pairs[2:6]:
+        copy.wait()
+
+    @pl.loop(0, 3)
+    def _(j):
+        n0 = pl.multiple_of(j * wide, wide)
+        hot = one_hot(n0, wide, index[:, two : 2 * two])
+        at = (slice(None), pl.ds(n0, wide))
+        spread[at] = (spread[at].astype(F32) - dot_nt(received[...], hot)).astype(BF16)
+
+    for copy in basis_copies:
+        copy.wait()
+    products = dot_nt(joint[...], spread[...]).astype(BF16)
+    mine = pl.ds(pl.multiple_of(b * four_cd, 16), four_cd)
+    loads[mine] = products[:four_cd]
+
+    def load_copy(k):
+        return pltpu.make_async_remote_copy(
+            src_ref=loads.at[mine],
+            dst_ref=loads.at[mine],
+            send_sem=load_send.at[k],
+            recv_sem=load_recv.at[k],
+            device_id=(a, lax.rem(b + k, ny)),
+            device_id_type=MESH,
+        )
+
+    pl.loop(1, ny)(lambda k: load_copy(k).start())
+
+    mine_a = pl.ds(pl.multiple_of(a * four_cd, 16), four_cd)
+    bilinear[mine_a] = products[four_cd:]
+
+    def bil_copy(k):
+        return pltpu.make_async_remote_copy(
+            src_ref=bilinear.at[mine_a],
+            dst_ref=bilinear.at[mine_a],
+            send_sem=bil_send.at[k],
+            recv_sem=bil_recv.at[k],
+            device_id=(lax.rem(a + k, nx), b),
+            device_id_type=MESH,
+        )
+
+    pl.loop(1, nx)(lambda k: bil_copy(k).start())
+
+    product[...] = jnp.zeros_like(product)
+
+    @pl.loop(0, 3)
+    def _(j):
+        at = (slice(None), pl.ds(pl.multiple_of(j * wide, wide), wide))
+        masked = tile[at].reshape(nblock, group, 16, wide) * mask_rows[:, :, at[1]][:, None]
+        full = dot(spread[...], masked.reshape(width, wide))
+        image[0:nrhs, at[1]] = full.astype(BF16)
+        full = full * spread[at].astype(F32)
+        total = product[...]
+        for q in range(wide // 128):
+            total = total + full[:, q * 128 : (q + 1) * 128]
+        product[...] = total
+
     pl.loop(1, ny)(lambda k: load_copy(k).wait())
     solution_part = dot(solve[...], loads[...])
     parts[...] = solution_part.astype(BF16)
@@ -334,13 +328,12 @@
     fine = lax.dot_general(
         jnp.ones((8, 128), F32), product[...], NT, precision=lax.Precision.HIGHEST, preferred_element_type=F32
     )
-    mine_y = pl.ds(pl.multiple_of(b * 8, 8), 8)
-    sum_y[mine_y] = fine - coarse
+    sum_y[b] = (fine - coarse)[0:1]
 
     def sumy_copy(k):
         return pltpu.make_async_remote_copy(
-            src_ref=sum_y.at[mine_y],
-            dst_ref=sum_y.at[mine_y],
+            src_ref=sum_y.at[b],
+            dst_ref=sum_y.at[b],
             send_sem=sumy_send.at[k],
             recv_sem=sumy_recv.at[k],
             device_id=(a, lax.rem(b + k, ny)),
@@ -348,6 +341,18 @@
         )
 
     pl.loop(1, ny)(lambda k: sumy_copy(k).start())
+
+    def gathered(first, count):
+        both = dot(image[...], one_hot(0, width, index[:, first : first + count])).astype(BF16)
+        return both[:nrhs], both[nrhs:]
+
+    west_pieces = []
+    for slot, first, count in ((10, 0, first_piece), (6, first_piece, faces - first_piece)):
+        at = (slice(None), slice(first, first + count))
+        face_out[at], basis_out[at] = gathered(two + first, count)
+        at = (slice(None), pl.ds(first, count))
+        west_pieces.append(send(face_out.at[at], face_in.at[at], slot, west))
+    pairs.append(west_pieces[1])
 
     face_out[:, faces:two], basis_out[:, faces:two] = gathered(two + faces, faces)
     pairs.append(send(face_out.at[:, south_half], face_in.at[:, south_half], 7, north))
@@ -356,13 +361,12 @@
     pairs.append(send(basis_out.at[:, south_half], stack.at[theirs, south_half], 9, north))
     face_own[...], stack[0:four_cd] = gathered(0, two)
     pl.loop(1, ny)(lambda k: sumy_copy(k).wait())
-    mine_x = pl.ds(pl.multiple_of(a * 8, 8), 8)
-    sum_x[mine_x] = jnp.sum(sum_y[...].reshape(ny, 8, nrhs), axis=0)
+    sum_x[a] = jnp.sum(sum_y[...], axis=0)
 
     def sumx_copy(k):
         return pltpu.make_async_remote_copy(
-            src_ref=sum_x.at[mine_x],
-            dst_ref=sum_x.at[mine_x],
+            src_ref=sum_x.at[a],
+            dst_ref=sum_x.at[a],
             send_sem=sumx_send.at[k],
             recv_sem=sumx_recv.at[k],
             device_id=(lax.rem(a + k, nx), b),
@@ -394,10 +398,10 @@
         corrections.append(dot(coefficient, stack[:, f * faces : (f + 1) * faces]))
 
     pl.loop(1, nx)(lambda k: sumx_copy(k).wait())
-    everything = jnp.sum(sum_x[...].reshape(nx, 8, nrhs), axis=0)
-    curvature_ref[...] = everything[0:1] / (2.0 * faces * nx * ny)
+    curvature_ref[...] = jnp.sum(sum_x[...], axis=0) / (2.0 * faces * nx * ny)
 
     pairs[7].wait()
+    west_pieces[0].wait()
     pairs[6].wait()
     for f in range(2):
         at = (slice(None), slice(f * faces, (f + 1) * faces))
@@ -467,11 +471,11 @@
             vmem((nrhs, two), BF16),
             vmem((nrhs, two), BF16),
             vmem((nrhs, two), BF16),
-            vmem((nx * 8, nrhs), F32),
-            vmem((ny * 8, nrhs), F32),
+            vmem((nx, 1, nrhs), F32),
+            vmem((ny, 1, nrhs), F32),
             dma((13,)),
-            dma((10,)),
-            dma((10,)),
+            dma((11,)),
+            dma((11,)),
             dma((ny,)),
             dma((ny,)),
             dma((nx,)),

time: 50.1 us -> 48.9 us (0.976)
  Pallas kernels: 49.3 us -> 48.2 us
    pallas_call x1, Pallas kernels: 47 us -> 45.8 us  [shards(): pl.pallas_call(functools.partial(kernel, nx, ny), out_shape=(jax.ShapeDty...]
where the time goes in v3:
time: 48.9 us; the launch traced here: 48.8 us
  Pallas kernels  48.2 us (99%)
  between operations  0.64 us (1%)
    pallas_call x1, Pallas kernels, shards(): pl.pallas_call(functools.partial(kernel, nx, ny), out_shape=(jax.ShapeDty...  45.8 us
    pallas_call x1, Pallas kernels, shards(): pl.pallas_call(finish, out_shape=(jax.ShapeDtypeStruct(lam.shape, BF16),...  2.32 us

profile of v3, /device:TPU:1, one launch (start us, length us, event | category | flops | bytes accessed | tf_op | source)
XLA Modules:
  0.0 48.8 jit_solution(4768762893886602666)
XLA Ops:
  0.6 45.8 %shard_map.86 = (bf16[256,1280]{1,0:T(8,128)(2,1)}, f32[1,256]{1,0:T(1,128)}) custom-call(bf16[256,2,640]{2,1,0:T(2,128)(2,1)} %bitcast.9, s32[2,640]{1,0:T(2,128)} %bitcast.13, s32[1,2608]{1,0:T(1,128)} %bitcast.11, s32[16,16]{1,0:T(8,128)} %bitcast.12, bf16[3072,3072]{1,0:T(8,128)(2,1)} %bitcast.8, bf16[48,3072]{1,0:T(8,128)(2,1)} %bitcast.10, ...), custom_call_target="tpu_custom_call" | custom-call | tf_op jit(solution)/shard_map/pallas_call | solution.py:439
  46.5 2.3 %shard_map.87 = (bf16[256,2,640]{2,1,0:T(2,128)(2,1)}, f32[1,256]{1,0:T(1,128)}) custom-call(bf16[256,1280]{1,0:T(8,128)(2,1)} %get-tuple-element.6.jump, f32[1,256]{1,0:T(1,128)} %get-tuple-element.7.curvature), custom_call_target="tpu_custom_call" | custom-call | tf_op jit(solution)/shard_map/pallas_call | solution.py:494

commit v4 on v3

--- a/solution.py
+++ b/solution.py
@@ -352,10 +352,12 @@
         face_out[at], basis_out[at] = gathered(two + first, count)
         at = (slice(None), pl.ds(first, count))
         west_pieces.append(send(face_out.at[at], face_in.at[at], slot, west))
+        if first == 0:
+            face_out[:, faces:two], basis_out[:, faces:two] = gathered(two + faces, faces)
+            north_copy = send(face_out.at[:, south_half], face_in.at[:, south_half], 7, north)
     pairs.append(west_pieces[1])
-
-    face_out[:, faces:two], basis_out[:, faces:two] = gathered(two + faces, faces)
-    pairs.append(send(face_out.at[:, south_half], face_in.at[:, south_half], 7, north))
+    pairs.append(north_copy)
+
     theirs = pl.ds(four_cd, four_cd)
     pairs.append(send(basis_out.at[:, east_half], stack.at[theirs, east_half], 8, west))
     pairs.append(send(basis_out.at[:, south_half], stack.at[theirs, south_half], 9, north))

time: 48.9 us -> 48.6 us (level)
  no operation moved by 1% of the time
where the time goes in v4:
time: 48.6 us; the launch traced here: 48.4 us
  Pallas kernels  47.8 us (98%)
  between operations  0.64 us (1%)
    pallas_call x1, Pallas kernels, shards(): pl.pallas_call(functools.partial(kernel, nx, ny), out_shape=(jax.ShapeDty...  45.5 us
    pallas_call x1, Pallas kernels, shards(): pl.pallas_call(finish, out_shape=(jax.ShapeDtypeStruct(lam.shape, BF16),...  2.32 us

profile of v4, /device:TPU:1, one launch (start us, length us, event | category | flops | bytes accessed | tf_op | source)
XLA Modules:
  0.0 48.4 jit_solution(16307061668995824655)
XLA Ops:
  0.6 45.5 %shard_map.86 = (bf16[256,1280]{1,0:T(8,128)(2,1)}, f32[1,256]{1,0:T(1,128)}) custom-call(bf16[256,2,640]{2,1,0:T(2,128)(2,1)} %bitcast.9, s32[2,640]{1,0:T(2,128)} %bitcast.13, s32[1,2608]{1,0:T(1,128)} %bitcast.11, s32[16,16]{1,0:T(8,128)} %bitcast.12, bf16[3072,3072]{1,0:T(8,128)(2,1)} %bitcast.8, bf16[48,3072]{1,0:T(8,128)(2,1)} %bitcast.10, ...), custom_call_target="tpu_custom_call" | custom-call | tf_op jit(solution)/shard_map/pallas_call | solution.py:441
  46.1 2.3 %shard_map.87 = (bf16[256,2,640]{2,1,0:T(2,128)(2,1)}, f32[1,256]{1,0:T(1,128)}) custom-call(bf16[256,1280]{1,0:T(8,128)(2,1)} %get-tuple-element.6.jump, f32[1,256]{1,0:T(1,128)} %get-tuple-element.7.curvature), custom_call_target="tpu_custom_call" | custom-call | tf_op jit(solution)/shard_map/pallas_call | solution.py:496
